TPU v7x, 32 devices: a whole 2x2x4 slice. The times are simulated.
32 devices in a mesh: section: 2 (over x), group: 4 (over z), narrow: 4 (over y, core).
Axes of the slice: x: 2, y: 2, z: 4, core: 2. Of those that a mesh axis runs over, the one named last changes fastest.
Arguments:
- boundary: bfloat16 [2, 8, 1024, 768], P('section', 'group', 'narrow'), may hold values from -6 to 6
- segments: int32 [8, 1024], P('group'), may hold values from 0 to 3, never falling along the last dimension, each value on 1 to 769 neighbouring positions
- qkv_weight: bfloat16 [2, 768, 2304], P('section'), may hold values from -0.21875 to 0.21875
- proj_weight: bfloat16 [2, 768, 768], P('section'), may hold values from -3 to 3
- fc1_weight: bfloat16 [2, 768, 3072], P('section'), may hold values from -0.21875 to 0.21875
- fc2_weight: bfloat16 [2, 3072, 768], P('section'), may hold values from -0.109375 to 0.109375
- gains: float32 [2, 4, 768], P('section'), may hold values from 0.5 to 1.5
- biases: float32 [2, 6, 768], P('section'), may hold values from -1.8 to 1.8
- fc1_bias: float32 [2, 3072], P('section'), may hold values from -1.8 to 1.8
Outputs:
- results: bfloat16 [2, 8, 1024, 768], P('section', 'group', 'narrow')
- grad_qkv: float32 [2, 768, 2304], P('section', 'narrow')
- grad_proj: float32 [2, 768, 768], P('section', 'narrow')
- grad_fc1: float32 [2, 768, 3072], P('section', 'narrow')
- grad_fc2: float32 [2, 3072, 768], P('section', 'narrow')
- grad_gains: float32 [2, 4, 768], P('section', None, 'narrow')
- grad_biases: float32 [2, 6, 768], P('section', None, 'narrow')
- grad_fc1_bias: float32 [2, 3072], P('section', 'narrow')
Inputs may be any that keep to these rules, and one draw needn't show every extreme that they name: `segments`: along each sequence the segment numbers never fall, every number 0 to 3 occurs, each image has 1 to 769 tokens and one image of every sequence has exactly 769.
All inputs are finite; a program needn't handle non-finite values.
Results may differ from a plain program's by a relative error of at most 0.014.
Values may be sent and summed in bfloat16 or wider, within the bound.
A program may use at most 256 MiB of HBM per device.

v0:
```python
import jax
import jax.numpy as jnp
from jax import lax
from jax.sharding import PartitionSpec as P

HEADS = 12
HDIM = 64


def from_behind(block, axis, distance):
    devices = range(lax.axis_size(axis))
    route = [(i - distance, i) for i in devices if i - distance in devices]
    return lax.ppermute(block, axis, route)


def normalize(values, scale_vec, shift_vec):
    row_mean = jnp.mean(values, -1, keepdims=True)
    centered = values - row_mean
    variance = jnp.mean(centered * centered, -1, keepdims=True)
    return centered * lax.rsqrt(variance + 1e-06) * scale_vec + shift_vec


def gelu_exact(values):
    return jax.nn.gelu(values, approximate=False)


def back_dot(left, weight):
    return lax.dot_general(
        left, weight, (((1,), (1,)), ((), ())), preferred_element_type=jnp.float32
    )


def row_contract(left, right):
    return lax.dot_general(
        left, right, (((0,), (0,)), ((), ())), preferred_element_type=jnp.float32
    )


def masked_scores(query, keys_all, seg_row):
    row_count = query.shape[0]
    length = keys_all.shape[0]
    start = lax.axis_index("narrow") * row_count
    own_seg = lax.dynamic_slice_in_dim(seg_row, start, row_count)
    same = own_seg[:, None] == seg_row[None, :]
    raw = (
        jnp.einsum(
            "qhd,khd->hqk",
            query.reshape(row_count, HEADS, HDIM),
            keys_all.reshape(length, HEADS, HDIM),
            preferred_element_type=jnp.float32,
        )
        * 0.125
    )
    return jnp.where(same[None], raw, -1e30)


def forward_layer(inputs, seg_row, weights):
    qkv_w, proj_w, fc1_w, fc2_w, gain_rows, bias_rows, fc1_b = weights
    row_count, model_width = inputs.shape
    normed = normalize(inputs, gain_rows[0], bias_rows[0]).astype(jnp.bfloat16)
    qkv = jnp.dot(normed, qkv_w, preferred_element_type=jnp.float32)
    query = (qkv[:, :model_width] + bias_rows[1]).astype(jnp.bfloat16)
    key_rows = qkv[:, model_width : 2 * model_width].astype(jnp.bfloat16)
    value_rows = (qkv[:, 2 * model_width :] + bias_rows[2]).astype(jnp.bfloat16)
    keys_all, values_all = (
        lax.all_gather(key_rows, "narrow", axis=0, tiled=True),
        lax.all_gather(value_rows, "narrow", axis=0, tiled=True),
    )
    length = keys_all.shape[0]
    scores = masked_scores(query, keys_all, seg_row)
    peak = jnp.max(scores, -1, keepdims=True)
    log_total = peak + jnp.log(jnp.sum(jnp.exp(scores - peak), -1, keepdims=True))
    probs = jnp.exp(scores - log_total).astype(jnp.bfloat16)
    mixed = jnp.einsum(
        "hqk,khd->qhd",
        probs,
        values_all.reshape(length, HEADS, HDIM),
        preferred_element_type=jnp.float32,
    )
    attended = mixed.reshape(row_count, model_width).astype(jnp.bfloat16)
    branch = jnp.dot(attended, proj_w, preferred_element_type=jnp.float32) + bias_rows[3]
    middle = inputs + gain_rows[1] * branch
    normed_two = normalize(middle, gain_rows[2], bias_rows[4]).astype(jnp.bfloat16)
    hidden_pre = jnp.dot(normed_two, fc1_w, preferred_element_type=jnp.float32) + fc1_b
    activated = gelu_exact(hidden_pre).astype(jnp.bfloat16)
    mlp_out = jnp.dot(activated, fc2_w, preferred_element_type=jnp.float32) + bias_rows[5]
    output = middle + gain_rows[3] * mlp_out
    saved = (
        inputs,
        query,
        keys_all,
        values_all,
        log_total,
        attended,
        branch,
        middle,
        hidden_pre,
        mlp_out,
    )
    return (output, saved)


def backward_layer(grad_out, saved, seg_row, weights):
    qkv_w, proj_w, fc1_w, fc2_w, gain_rows, bias_rows, fc1_b = weights
    (
        inputs,
        query,
        keys_all,
        values_all,
        log_total,
        attended,
        branch,
        middle,
        hidden_pre,
        mlp_out,
    ) = saved
    row_count, model_width = inputs.shape
    length = keys_all.shape[0]
    scale_two = jnp.sum(grad_out * mlp_out, 0)
    mlp_grad = (gain_rows[3] * grad_out).astype(jnp.bfloat16)
    activated, gelu_pull = jax.vjp(gelu_exact, hidden_pre)
    grad_fc2 = row_contract(activated.astype(jnp.bfloat16), mlp_grad)
    shift_five = jnp.sum(mlp_grad.astype(jnp.float32), 0)
    pre_grad = gelu_pull(back_dot(mlp_grad, fc2_w))[0].astype(jnp.bfloat16)
    normed_two, norm_pull_two = jax.vjp(normalize, middle, gain_rows[2], bias_rows[4])
    grad_fc1 = row_contract(normed_two.astype(jnp.bfloat16), pre_grad)
    grad_fc1b = jnp.sum(pre_grad.astype(jnp.float32), 0)
    middle_part, gain_two, shift_four = norm_pull_two(back_dot(pre_grad, fc1_w))
    middle_grad = grad_out + middle_part
    scale_one = jnp.sum(middle_grad * branch, 0)
    branch_grad = (gain_rows[1] * middle_grad).astype(jnp.bfloat16)
    grad_proj = row_contract(attended, branch_grad)
    shift_three = jnp.sum(branch_grad.astype(jnp.float32), 0)
    heads_grad = back_dot(branch_grad, proj_w).astype(jnp.bfloat16).reshape(row_count, HEADS, HDIM)
    scores = masked_scores(query, keys_all, seg_row)
    probs = jnp.exp(scores - log_total)
    keys_heads = keys_all.reshape(length, HEADS, HDIM)
    prob_grad = jnp.einsum(
        "qhd,khd->hqk",
        heads_grad,
        values_all.reshape(length, HEADS, HDIM),
        preferred_element_type=jnp.float32,
    )
    inner = jnp.sum(probs * prob_grad, -1, keepdims=True)
    score_grad = (probs * (prob_grad - inner)).astype(jnp.bfloat16)
    query_grad = (
        (
            jnp.einsum("hqk,khd->qhd", score_grad, keys_heads, preferred_element_type=jnp.float32)
            * 0.125
        )
        .reshape(row_count, model_width)
        .astype(jnp.bfloat16)
    )
    key_part = (
        jnp.einsum(
            "hqk,qhd->khd",
            score_grad,
            query.reshape(row_count, HEADS, HDIM),
            preferred_element_type=jnp.float32,
        )
        * 0.125
    ).reshape(length, model_width)
    value_part = jnp.einsum(
        "hqk,qhd->khd", probs.astype(jnp.bfloat16), heads_grad, preferred_element_type=jnp.float32
    ).reshape(length, model_width)
    key_sum, value_sum = (
        lax.psum_scatter(
            key_part.astype(jnp.bfloat16), "narrow", scatter_dimension=0, tiled=True
        ).astype(jnp.float32),
        lax.psum_scatter(
            value_part.astype(jnp.bfloat16), "narrow", scatter_dimension=0, tiled=True
        ).astype(jnp.float32),
    )
    key_grad = key_sum.astype(jnp.bfloat16)
    value_grad = value_sum.astype(jnp.bfloat16)
    qkv_grad = jnp.concatenate([query_grad, key_grad, value_grad], 1)
    normed, norm_pull_one = jax.vjp(normalize, inputs, gain_rows[0], bias_rows[0])
    grad_qkv = row_contract(normed.astype(jnp.bfloat16), qkv_grad)
    input_part, gain_one, shift_zero = norm_pull_one(back_dot(qkv_grad, qkv_w))
    input_grad = middle_grad + input_part
    gain_grads = jnp.stack([gain_one, scale_one, gain_two, scale_two])
    shift_grads = jnp.stack(
        [
            shift_zero,
            jnp.sum(query_grad.astype(jnp.float32), 0),
            jnp.sum(value_grad.astype(jnp.float32), 0),
            shift_three,
            shift_four,
            shift_five,
        ]
    )
    return (
        input_grad,
        (grad_qkv, grad_proj, grad_fc1, grad_fc2, gain_grads, shift_grads, grad_fc1b),
    )


def body(
    boundary, segments, qkv_weight, proj_weight, fc1_weight, fc2_weight, gains, biases, fc1_bias
):
    weights = (
        qkv_weight[0],
        proj_weight[0],
        fc1_weight[0],
        fc2_weight[0],
        gains[0],
        biases[0],
        fc1_bias[0],
    )
    local_ends = boundary[0]
    micro_count = local_ends.shape[0]
    first_section = lax.axis_index("section") == 0
    arrived = jnp.zeros(local_ends.shape[1:], jnp.bfloat16)
    stored = []
    outputs = []
    for step_index in range(micro_count + 1):
        lower = min(step_index, micro_count - 1)
        upper = max(step_index - 1, 0)
        inputs = jnp.where(
            first_section, local_ends[lower].astype(jnp.float32), arrived.astype(jnp.float32)
        )
        seg_row = jnp.where(first_section, segments[lower], segments[upper])
        output, saved = forward_layer(inputs, seg_row, weights)
        stored.append((saved, seg_row))
        outputs.append(output)
        if step_index < micro_count:
            arrived = from_behind(output.astype(jnp.bfloat16), "section", 1)
    totals = tuple((jnp.zeros(w.shape, jnp.float32) for w in weights))
    returned = jnp.zeros(local_ends.shape[1:], jnp.bfloat16)
    input_grads = []
    for step_index in range(micro_count + 1):
        lower = min(step_index, micro_count - 1)
        upper = max(step_index - 1, 0)
        picked = jax.tree.map(
            lambda early, later: jnp.where(first_section, early, later),
            stored[upper],
            stored[lower + 1],
        )
        cotangent = jnp.where(
            first_section, returned.astype(jnp.float32), local_ends[lower].astype(jnp.float32)
        )
        is_valid = jnp.where(first_section, step_index >= 1, step_index < micro_count)
        cotangent = jnp.where(is_valid, cotangent, 0.0)
        grad_in, pieces = backward_layer(cotangent, picked[0], picked[1], weights)
        totals = tuple((acc + part for acc, part in zip(totals, pieces)))
        input_grads.append(grad_in)
        if step_index < micro_count:
            returned = from_behind(grad_in.astype(jnp.bfloat16), "section", -1)
    results = jnp.stack(
        [jnp.where(first_section, input_grads[j + 1], outputs[j + 1]) for j in range(micro_count)]
    )
    results = results.astype(jnp.bfloat16)
    within = (
        lax.psum_scatter(
            totals[0].astype(jnp.bfloat16), "narrow", scatter_dimension=0, tiled=True
        ).astype(jnp.float32),
        lax.psum_scatter(
            totals[1].astype(jnp.bfloat16), "narrow", scatter_dimension=0, tiled=True
        ).astype(jnp.float32),
        lax.psum_scatter(
            totals[2].astype(jnp.bfloat16), "narrow", scatter_dimension=0, tiled=True
        ).astype(jnp.float32),
        lax.psum_scatter(
            totals[3].astype(jnp.bfloat16), "narrow", scatter_dimension=0, tiled=True
        ).astype(jnp.float32),
        lax.psum_scatter(
            totals[4].astype(jnp.bfloat16), "narrow", scatter_dimension=1, tiled=True
        ).astype(jnp.float32),
        lax.psum_scatter(
            totals[5].astype(jnp.bfloat16), "narrow", scatter_dimension=1, tiled=True
        ).astype(jnp.float32),
        lax.psum_scatter(
            totals[6].astype(jnp.bfloat16), "narrow", scatter_dimension=0, tiled=True
        ).astype(jnp.float32),
    )
    final = (
        lax.psum(within[0].astype(jnp.bfloat16), "group").astype(jnp.float32),
        lax.psum(within[1].astype(jnp.bfloat16), "group").astype(jnp.float32),
        lax.psum(within[2].astype(jnp.bfloat16), "group").astype(jnp.float32),
        lax.psum(within[3].astype(jnp.bfloat16), "group").astype(jnp.float32),
        lax.psum(within[4].astype(jnp.bfloat16), "group").astype(jnp.float32),
        lax.psum(within[5].astype(jnp.bfloat16), "group").astype(jnp.float32),
        lax.psum(within[6].astype(jnp.bfloat16), "group").astype(jnp.float32),
    )
    return (
        results[None],
        final[0][None],
        final[1][None],
        final[2][None],
        final[3][None],
        final[4][None],
        final[5][None],
        final[6][None],
    )


def solution(mesh):
    placed = (
        P("section", "group", "narrow", None),
        P("group", None),
        P("section", None, None),
        P("section", None, None),
        P("section", None, None),
        P("section", None, None),
        P("section", None, None),
        P("section", None, None),
        P("section", None),
    )
    return jax.shard_map(
        body,
        mesh=mesh,
        in_specs=placed,
        out_specs=(
            P("section", "group", "narrow", None),
            P("section", "narrow", None),
            P("section", "narrow", None),
            P("section", "narrow", None),
            P("section", "narrow", None),
            P("section", None, "narrow"),
            P("section", None, "narrow"),
            P("section", "narrow"),
        ),
        check_vma=False,
    )
```

profile of v0, /device:TPU:0, one launch (start us, length us, event | category | flops | bytes accessed | tf_op | source)
XLA Modules:
  0.0 979.3 jit_solution(14836901581600981948)
XLA Ops:
  25.0 14.6 %all-gather.9.cloned.1.call-done = bf16[1024,768]{1,0:T(8,128)(2,1)} async-done(((bf16[256,768]{1,0:T(8,128)(2,1)}), bf16[1024,768]{1,0:T(8,128)(2,1)}) %all-gather.9.cloned.1.call-update) | async-done | bytes 1572880 | tf_op jit(solution)/shard_map/all_gather | solution.py:66
  51.4 10.1 %all-gather.7.cloned.1.call-done = bf16[1024,768]{1,0:T(8,128)(2,1)} async-done(((bf16[256,768]{1,0:T(8,128)(2,1)}), bf16[1024,768]{1,0:T(8,128)(2,1)}) %all-gather.7.cloned.1.call-update) | async-done | bytes 1572880 | tf_op jit(solution)/shard_map/all_gather | solution.py:67
  64.1 8.1 fusion.244
  76.1 9.0 add_convert_fusion.18
  88.5 8.7 collective-permute-done
  113.9 9.1 all-gather.13.cloned.1.call-done
  140.2 4.5 all-gather.11.cloned.1.call-done
  147.3 8.1 fusion.243
  166.4 11.6 %convert_reduce_fusion.2 = (f32[3072]{0:T(1024)}, bf16[256,3072]{1,0:T(8,128)(2,1)S(1)}) fusion(bf16[1,3072,768]{2,1,0:T(8,128)(2,1)} %param.14, f32[768]{0:T(1024)S(1)} %copy-done.114, pred[]{:T(512)S(6)} %eq.109, pred[]{:T(512)S(6)} %select_n.313, bf16[1,2,256,768]{3,2,1,0:T(8,128)(2,1)S(1)} %copy-done.8, f32[256,3072]{1,0:T(8,128)S(1)} %copy-done.178, ...), kind=kOutput, calls=%fused_computation.98 | convolution fusion | flops 1267921920 | bytes 12994048 | tf_op jit(solution)/shard_map/dot_general | solution.py:28
  194.3 8.1 multiply_reduce_fusion.2
  202.4 6.7 multiply_convert_fusion.2
  213.8 9.2 fusion.120
  225.6 11.9 %fusion.354 = (bf16[256,768]{1,0:T(8,128)(2,1)}, f32[256,768]{1,0:T(8,128)}) fusion(f32[256,768]{1,0:T(8,128)} %get-tuple-element.104, f32[768]{0:T(1024)} %get-tuple-element.48, f32[768]{0:T(1024)} %get-tuple-element.42, bf16[1,3072,768]{2,1,0:T(8,128)(2,1)} %param.14, f32[256,3072]{1,0:T(8,128)} %copy-done.180), kind=kOutput, calls=%fused_computation.528 | convolution fusion | flops 1259864064 | bytes 9836544 | tf_op jit(solution)/shard_map/dot_general | solution.py:86
  241.7 6.2 convert_reduce_fusion.14
  247.9 24.1 %reduce-scatter.19.cloned.1.call-done = bf16[256,768]{0,1:T(8,128)(2,1)} async-done(((bf16[1024,768]{0,1:T(8,128)(2,1)}), bf16[256,768]{0,1:T(8,128)(2,1)}) %reduce-scatter.19.cloned.1.call-update) | async-done | bytes 393232 | tf_op jit(solution)/shard_map/reduce_scatter | solution.py:170
  281.1 11.2 %collective-permute-done.1 = bf16[256,768]{1,0:T(8,128)(2,1)S(1)} collective-permute-done((bf16[256,768]{1,0:T(8,128)(2,1)S(1)}, bf16[256,768]{1,0:T(8,128)(2,1)S(1)}, u32[]{:S(2)}, u32[]{:S(2)}) %collective-permute-start.1) | collective-permute-done | bytes 393248 | tf_op jit(solution)/shard_map/ppermute | solution.py:13
  311.6 7.2 all-gather.17.cloned.1.call-done
  325.7 14.4 %all-gather.15.cloned.1.call-done = bf16[1024,768]{1,0:T(8,128)(2,1)} async-done(((bf16[256,768]{1,0:T(8,128)(2,1)}), bf16[1024,768]{1,0:T(8,128)(2,1)}) %all-gather.15.cloned.1.call-update) | async-done | bytes 1572880 | tf_op jit(solution)/shard_map/all_gather | solution.py:67
  362.4 7.9 broadcast_select_fusion.9
  378.1 4.3 fusion.51
  382.7 11.6 %convert_reduce_fusion.1 = (f32[3072]{0:T(1024)}, bf16[256,3072]{1,0:T(8,128)(2,1)S(1)}) fusion(bf16[256,768]{1,0:T(8,128)(2,1)S(1)} %copy-done.103, bf16[1,3072,768]{2,1,0:T(8,128)(2,1)} %param.14, f32[256,3072]{1,0:T(8,128)S(1)} %copy-done.179, f32[256,3072]{1,0:T(8,128)S(1)} %fusion.51, pred[]{:T(512)S(6)} %eq.109), kind=kOutput, calls=%fused_computation.97 | convolution fusion | flops 1266938880 | bytes 12988417 | tf_op jit(solution)/shard_map/dot_general | solution.py:28
  406.2 8.1 multiply_reduce_fusion.1
  414.3 6.9 multiply_convert_fusion.1
  434.5 9.0 fusion.123
  443.6 6.8 convert_reduce_fusion.10
  450.5 6.4 fusion.508
  456.9 8.8 fusion.237
  465.7 17.5 %reduce-scatter.23.cloned.1.call-done = bf16[256,768]{0,1:T(8,128)(2,1)} async-done(((bf16[1024,768]{0,1:T(8,128)(2,1)}), bf16[256,768]{0,1:T(8,128)(2,1)}) %reduce-scatter.23.cloned.1.call-update) | async-done | bytes 393232 | tf_op jit(solution)/shard_map/reduce_scatter | solution.py:170
  493.8 7.6 collective-permute-done.3
  503.3 11.2 %convert_reduce_fusion = (f32[3072]{0:T(1024)}, bf16[256,3072]{1,0:T(8,128)(2,1)S(1)}) fusion(bf16[256,768]{1,0:T(8,128)(2,1)S(1)} %get-tuple-element.68, bf16[1,3072,768]{2,1,0:T(8,128)(2,1)} %param.14, f32[256,3072]{1,0:T(8,128)} %copy-done.180, f32[256,3072]{1,0:T(8,128)} %copy-done.181, pred[]{:T(512)S(6)} %eq.109), kind=kOutput, calls=%fused_computation.96 | convolution fusion | flops 1266938880 | bytes 12988417 | tf_op jit(solution)/shard_map/dot_general | solution.py:28
  514.6 5.2 multiply_reduce_fusion.4
  528.2 12.1 %multiply_reduce_fusion = (f32[12,256]{1,0:T(8,128)S(1)}, f32[12,256,1024]{2,1,0:T(8,128)}) fusion(f32[12,256,1024]{2,1,0:T(8,128)} %fusion.508, f32[12,256]{1,0:T(8,128)} %get-tuple-element.75, pred[256,1024]{1,0:T(8,128)(4,1)} %broadcast_compare_fusion, bf16[256,12,64]{0,2,1:T(8,128)(2,1)} %bitcast.371, bf16[1024,12,64]{0,2,1:T(8,128)(2,1)} %bitcast.344), kind=kOutput, calls=%fused_computation.1 | convolution fusion | flops 418378752 | bytes 27418624 | tf_op jit(solution)/shard_map/qhd,khd->hqk/dot_general | solution.py:138
  541.5 7.2 multiply_convert_fusion
  552.0 12.1 %fusion.132 = f32[3072,768]{1,0:T(8,128)} fusion(f32[768]{0:T(1024)S(1)} %copy-done.116, pred[]{:T(512)S(6)} %eq.109, pred[]{:T(512)S(6)} %select_n.313, bf16[1,2,256,768]{3,2,1,0:T(8,128)(2,1)} %param.9, f32[256,3072]{1,0:T(8,128)} %copy-done.177, f32[256,3072]{1,0:T(8,128)} %copy-done.180), kind=kOutput, calls=%fused_computation.196 | convolution fusion | flops 1260847104 | bytes 16126464 | tf_op jit(solution)/shard_map/dot_general | solution.py:34
  564.1 8.1 fusion.126
  576.0 12.0 %fusion.133 = f32[3072,768]{1,0:T(8,128)} fusion(bf16[256,768]{1,0:T(8,128)(2,1)} %copy-done.104, f32[256,3072]{1,0:T(8,128)} %copy-done.180, f32[256,3072]{1,0:T(8,128)} %copy-done.181, pred[]{:T(512)S(6)} %eq.109), kind=kOutput, calls=%fused_computation.197 | convolution fusion | flops 1259864064 | bytes 16121857 | tf_op jit(solution)/shard_map/dot_general | solution.py:34
  588.1 14.4 %add_convert_fusion = bf16[3072,768]{1,0:T(8,128)(2,1)} fusion(f32[3072,768]{1,0:T(8,128)} %fusion.133, f32[3072,768]{1,0:T(8,128)} %fusion.132, bf16[256,768]{1,0:T(8,128)(2,1)} %get-tuple-element.61, f32[256,3072]{1,0:T(8,128)} %copy-done.177, f32[256,3072]{1,0:T(8,128)} %copy-done.181, pred[]{:T(512)S(6)} %eq.109), kind=kOutput, calls=%fused_computation.21 | convolution fusion | flops 1266941952 | bytes 30277632 | tf_op jit(solution)/shard_map/dot_general | solution.py:34
  606.7 5.2 fusion.291
  611.9 7.8 add_convert_fusion.1
  623.2 5.8 fusion.287
  636.6 8.8 add_convert_fusion.2
  694.3 45.4 %reduce-scatter.33.cloned.1.call-done = bf16[192,3072]{1,0:T(8,128)(2,1)} async-done(((bf16[768,3072]{1,0:T(8,128)(2,1)}), bf16[192,3072]{1,0:T(8,128)(2,1)}) %reduce-scatter.33.cloned.1.call-update) | async-done | bytes 1179664 | tf_op jit(solution)/shard_map/reduce_scatter | solution.py:260
  739.7 43.1 %reduce-scatter.29.cloned.1.call-done = bf16[192,2304]{1,0:T(8,128)(2,1)} async-done(((bf16[768,2304]{1,0:T(8,128)(2,1)}), bf16[192,2304]{1,0:T(8,128)(2,1)}) %reduce-scatter.29.cloned.1.call-update) | async-done | bytes 884752 | tf_op jit(solution)/shard_map/reduce_scatter | solution.py:254
  785.5 6.4 all-reduce
  797.9 7.5 reduce-scatter.37.cloned.1.call-done
  806.3 21.7 %reduce-scatter.39.cloned.1.call-done = bf16[192,6]{1,0:T(8,128)(2,1)} async-done(((bf16[768,6]{1,0:T(8,128)(2,1)}), bf16[192,6]{1,0:T(8,128)(2,1)}) %reduce-scatter.39.cloned.1.call-update) | async-done | bytes 2320
  828.9 12.9 %all-reduce.1 = (bf16[1,6,192]{2,1,0:T(8,128)(2,1)S(1)}, bf16[1,4,192]{2,1,0:T(4,128)(2,1)}, bf16[1,768]{1,0:T(2,128)(2,1)}) all-reduce(bf16[1,6,192]{2,1,0:T(8,128)(2,1)S(1)} %bitcast.395, bf16[1,4,192]{2,1,0:T(4,128)(2,1)S(1)} %bitcast.396, ...), channel_id=1, replica_groups=mesh['section'=2,'group'=4,'narrow'=4] {'group'}, use_global_device_ids=true, to_apply=%region_92.93 | all-reduce | flops 2688 | bytes 10752 | tf_op jit(solution)/shard_map/psum | solution.py:282
  845.0 120.7 %all-reduce.5.cloned.1.call-done = (bf16[1,192,2304]{2,1,0:T(8,128)(2,1)}, bf16[1,192,768]{2,1,0:T(8,128)(2,1)}, bf16[1,192,3072]{2,1,0:T(8,128)(2,1)}, bf16[1,768,768]{2,1,0:T(8,128)(2,1)}) async-done(((bf16[1,192,2304]{2,1,0:T(8,128)(2,1)}, bf16[1,192,768]{2,1,0:T(8,128)(2,1)}, bf16[1,192,3072]{2,1,0:T(8,128)(2,1)}, bf16[1,768,768]{2,1,0:T(8,128)(2,1)}), (bf16[1,192,2304]{2,1,0:T(8,128)(2,1)}, ...) | async-done | bytes 3538960 | tf_op jit(solution)/shard_map/psum | solution.py:277
  (656 shorter events, 316.6 us)
Async XLA Ops:
  7.2 32.4 %all-gather.9.cloned.1.call-start = ((), (), s32[]{:S(2)}) async-start(), calls=%async_computation.13 | async-start | bytes 1966080 | tf_op jit(solution)/shard_map/all_gather | solution.py:66
  11.3 475.5 %copy-start.91 = (f32[768]{0:T(1024)}, f32[768]{0:T(1024)S(1)}, u32[]{:S(2)}) copy-start(f32[768]{0:T(1024)S(1)} %get-tuple-element.49) | copy-start | bytes 9220
  12.7 282.5 %copy-start.95 = (f32[768]{0:T(1024)}, f32[768]{0:T(1024)S(1)}, u32[]{:S(2)}) copy-start(f32[768]{0:T(1024)S(1)} %get-tuple-element.46) | copy-start | bytes 9220
  12.7 365.4 %copy-start.97 = (f32[768]{0:T(1024)}, f32[768]{0:T(1024)S(1)}, u32[]{:S(2)}) copy-start(f32[768]{0:T(1024)S(1)} %get-tuple-element.47) | copy-start | bytes 9220
  17.1 44.3 %all-gather.7.cloned.1.call-start = ((), (), s32[]{:S(2)}) async-start(), calls=%async_computation.12 | async-start | bytes 1966080 | tf_op jit(solution)/shard_map/all_gather | solution.py:67
  19.5 103.4 %all-gather.13.cloned.1.call-start = ((), (), s32[]{:S(2)}) async-start(), calls=%async_computation.15 | async-start | bytes 1966080 | tf_op jit(solution)/shard_map/all_gather | solution.py:66
  85.1 12.1 %collective-permute-start = (bf16[256,768]{1,0:T(8,128)(2,1)S(1)}, bf16[256,768]{1,0:T(8,128)(2,1)S(1)}, u32[]{:S(2)}, u32[]{:S(2)}) collective-permute-start(bf16[256,768]{1,0:T(8,128)(2,1)S(1)} %get-tuple-element.144), channel_id=1, source_target_pairs={{0,16},{1,17},{2,18},{3,19},{4,20},{5,21},{6,22},{7,23},{8,24},{9,... | collective-permute-start | bytes 1179656 | tf_op jit(solution)/shard_map/ppermute | solution.py:13
  102.2 42.5 %all-gather.11.cloned.1.call-start = ((), (), s32[]{:S(2)}) async-start(), calls=%async_computation.14 | async-start | bytes 1966080 | tf_op jit(solution)/shard_map/all_gather | solution.py:67
  106.1 141.8 %reduce-scatter.17.cloned.1.call-start = ((), (), s32[]{:S(2)}) async-start(), calls=%async_computation.16 | async-start | bytes 1966080 | tf_op jit(solution)/shard_map/reduce_scatter | solution.py:167
  161.9 16.1 %slice-start.11 = ((s8[4718592]{0:T(1024)(128)(4,1)}), s8[4194304]{0:T(1024)(128)(4,1)S(1)}, s32[]{:S(2)}) async-start(s8[4718592]{0:T(1024)(128)(4,1)} %bitcast.405), calls=%async_computation.42 | async-start | bytes 8388608
  166.1 11.9 %copy-start.180 = (f32[256,3072]{1,0:T(8,128)}, f32[256,3072]{1,0:T(8,128)S(1)}, u32[]{:S(2)}) copy-start(f32[256,3072]{1,0:T(8,128)S(1)} %fusion.48) | copy-start | bytes 9437188
  166.1 14.1 %copy-start.132 = (f32[256]{0:T(256)}, f32[256]{0:T(256)S(1)}, u32[]{:S(2)}) copy-start(f32[256]{0:T(256)S(1)} %broadcast_multiply_fusion.7) | copy-start | bytes 3076
  166.4 13.8 %copy-start.146 = (f32[256]{0:T(256)}, f32[256]{0:T(256)S(1)}, u32[]{:S(2)}) copy-start(f32[256]{0:T(256)S(1)} %fusion.359) | copy-start | bytes 3076
  166.4 11.6 %slice-start.12 = ((s8[4718592]{0:T(1024)(128)(4,1)}), s8[524288]{0:T(1024)(128)(4,1)S(1)}, s32[]{:S(2)}) async-start(s8[4718592]{0:T(1024)(128)(4,1)} %bitcast.405), calls=%async_computation.43 | async-start | bytes 1048576
  212.3 59.7 %reduce-scatter.19.cloned.1.call-start = ((), (), s32[]{:S(2)}) async-start(), calls=%async_computation.17 | async-start | bytes 1966080 | tf_op jit(solution)/shard_map/reduce_scatter | solution.py:170
  223.1 95.8 %all-gather.17.cloned.1.call-start = ((), (), s32[]{:S(2)}) async-start(), calls=%async_computation.19 | async-start | bytes 1966080 | tf_op jit(solution)/shard_map/all_gather | solution.py:66
  225.6 16.0 %copy-start.26 = (bf16[1024,768]{0,1:T(8,128)(2,1)S(1)}, bf16[1024,768]{0,1:T(8,128)(2,1)}, u32[]{:S(2)}) copy-start(bf16[1024,768]{0,1:T(8,128)(2,1)} %copy.74) | copy-start | bytes 4718596
  237.6 38.4 %collective-permute-start.2 = (bf16[256,768]{1,0:T(8,128)(2,1)}, bf16[256,768]{1,0:T(8,128)(2,1)}, u32[]{:S(2)}, u32[]{:S(2)}) collective-permute-start(bf16[256,768]{1,0:T(8,128)(2,1)} %get-tuple-element.149), channel_id=1, source_target_pairs={{0,16},{1,17},{2,18},{3,19},{4,20},{5,21},{6,22},{7,23},{8,24},{9,... | collective-permute-start | bytes 1179656 | tf_op jit(solution)/shard_map/ppermute | solution.py:13
  279.6 12.7 %collective-permute-start.1 = (bf16[256,768]{1,0:T(8,128)(2,1)S(1)}, bf16[256,768]{1,0:T(8,128)(2,1)S(1)}, u32[]{:S(2)}, u32[]{:S(2)}) collective-permute-start(bf16[256,768]{1,0:T(8,128)(2,1)S(1)} %get-tuple-element.113), channel_id=1, source_target_pairs={{16,0},{17,1},{18,2},{19,3},{20,4},{21,5},{22,6},{23,7},{24,8},{25... | collective-permute-start | bytes 1179656 | tf_op jit(solution)/shard_map/ppermute | solution.py:13
  300.0 40.2 %all-gather.15.cloned.1.call-start = ((), (), s32[]{:S(2)}) async-start(), calls=%async_computation.18 | async-start | bytes 1966080 | tf_op jit(solution)/shard_map/all_gather | solution.py:67
  302.0 163.7 %reduce-scatter.21.cloned.1.call-start = ((), (), s32[]{:S(2)}) async-start(), calls=%async_computation.20 | async-start | bytes 1966080 | tf_op jit(solution)/shard_map/reduce_scatter | solution.py:167
  378.0 18.5 %copy-start.35 = (f32[256,768]{1,0:T(8,128)}, f32[256,768]{1,0:T(8,128)S(1)}, u32[]{:S(2)}) copy-start(f32[256,768]{1,0:T(8,128)S(1)} %get-tuple-element.91) | copy-start | bytes 2359300
  378.1 16.2 %slice-start.13 = ((s8[4718592]{0:T(1024)(128)(4,1)}), s8[4194304]{0:T(1024)(128)(4,1)S(1)}, s32[]{:S(2)}) async-start(s8[4718592]{0:T(1024)(128)(4,1)} %bitcast.407), calls=%async_computation.44 | async-start | bytes 8388608
  382.4 11.9 %copy-start.181 = (f32[256,3072]{1,0:T(8,128)}, f32[256,3072]{1,0:T(8,128)S(1)}, u32[]{:S(2)}) copy-start(f32[256,3072]{1,0:T(8,128)S(1)} %fusion.51) | copy-start | bytes 9437188
  382.4 14.1 %copy-start.136 = (f32[256]{0:T(256)}, f32[256]{0:T(256)S(1)}, u32[]{:S(2)}) copy-start(f32[256]{0:T(256)S(1)} %broadcast_multiply_fusion.3) | copy-start | bytes 3076
  382.7 13.9 %copy-start.148 = (f32[256]{0:T(256)}, f32[256]{0:T(256)S(1)}, u32[]{:S(2)}) copy-start(f32[256]{0:T(256)S(1)} %fusion.361) | copy-start | bytes 3076
  424.4 58.7 %reduce-scatter.23.cloned.1.call-start = ((), (), s32[]{:S(2)}) async-start(), calls=%async_computation.21 | async-start | bytes 1966080 | tf_op jit(solution)/shard_map/reduce_scatter | solution.py:170
  443.5 193.1 %reduce-scatter.25.cloned.1.call-start = ((), (), s32[]{:S(2)}) async-start(), calls=%async_computation.22 | async-start | bytes 1966080 | tf_op jit(solution)/shard_map/reduce_scatter | solution.py:167
  443.6 13.2 %slice-start.7 = ((s8[4718592]{0:T(1024)(128)(4,1)}), s8[4194304]{0:T(1024)(128)(4,1)S(1)}, s32[]{:S(2)}) async-start(s8[4718592]{0:T(1024)(128)(4,1)} %bitcast.401), calls=%async_computation.38 | async-start | bytes 8388608
  488.3 13.1 %collective-permute-start.3 = (bf16[256,768]{1,0:T(8,128)(2,1)}, bf16[256,768]{1,0:T(8,128)(2,1)}, u32[]{:S(2)}, u32[]{:S(2)}) collective-permute-start(bf16[256,768]{1,0:T(8,128)(2,1)} %get-tuple-element.112), channel_id=1, source_target_pairs={{16,0},{17,1},{18,2},{19,3},{20,4},{21,5},{22,6},{23,7},{24,8},{25... | collective-permute-start | bytes 1179656 | tf_op jit(solution)/shard_map/ppermute | solution.py:13
  489.6 30.2 %copy-start.143 = (f32[256]{0:T(256)}, f32[256]{0:T(256)S(1)}, u32[]{:S(2)}) copy-start(f32[256]{0:T(256)S(1)} %broadcast_multiply_fusion.1) | copy-start | bytes 3076
  493.8 26.0 %copy-start.163 = (f32[256]{0:T(256)}, f32[256]{0:T(256)S(1)}, u32[]{:S(2)}) copy-start(f32[256]{0:T(256)S(1)} %fusion.363) | copy-start | bytes 3076
  528.2 12.2 %slice-start = ((s8[12582912]{0:T(1024)(128)(4,1)}), s8[4194304]{0:T(1024)(128)(4,1)S(1)}, s32[]{:S(2)}) async-start(s8[12582912]{0:T(1024)(128)(4,1)} %bitcast.327), calls=%async_computation.31 | async-start | bytes 8388608
  528.2 12.2 %slice-start.1 = ((s8[12582912]{0:T(1024)(128)(4,1)}), s8[4194304]{0:T(1024)(128)(4,1)S(1)}, s32[]{:S(2)}) async-start(s8[12582912]{0:T(1024)(128)(4,1)} %bitcast.327), calls=%async_computation.32 | async-start | bytes 8388608
  528.2 13.3 %slice-start.2 = ((s8[12582912]{0:T(1024)(128)(4,1)}), s8[4194304]{0:T(1024)(128)(4,1)S(1)}, s32[]{:S(2)}) async-start(s8[12582912]{0:T(1024)(128)(4,1)} %bitcast.327), calls=%async_computation.33 | async-start | bytes 8388608
  528.2 13.3 %copy-start.75 = (pred[256,1024]{1,0:T(8,128)(4,1)S(1)}, pred[256,1024]{1,0:T(8,128)(4,1)}, u32[]{:S(2)}) copy-start(pred[256,1024]{1,0:T(8,128)(4,1)} %broadcast_compare_fusion) | copy-start | bytes 786436
  528.2 13.3 %copy-start.117 = (f32[12,256]{1,0:T(8,128)S(1)}, f32[12,256]{1,0:T(8,128)}, u32[]{:S(2)}) copy-start(f32[12,256]{1,0:T(8,128)} %get-tuple-element.75) | copy-start | bytes 36868
  552.0 84.7 %reduce-scatter.27.cloned.1.call-start = ((), (), s32[]{:S(2)}) async-start(), calls=%async_computation.23 | async-start | bytes 1966080 | tf_op jit(solution)/shard_map/reduce_scatter | solution.py:170
  552.0 12.1 %copy-start.76 = (pred[256,1024]{1,0:T(8,128)(4,1)S(1)}, pred[256,1024]{1,0:T(8,128)(4,1)}, u32[]{:S(2)}) copy-start(pred[256,1024]{1,0:T(8,128)(4,1)} %broadcast_compare_fusion) | copy-start | bytes 786436
  552.0 12.1 %copy-start.89 = (bf16[256,768]{0,1:T(8,128)(2,1)S(1)}, bf16[256,768]{0,1:T(8,128)(2,1)}, u32[]{:S(2)}) copy-start(bf16[256,768]{0,1:T(8,128)(2,1)} %copy.87) | copy-start | bytes 1179652
  552.0 12.1 %copy-start.118 = (f32[12,256]{1,0:T(8,128)S(1)}, f32[12,256]{1,0:T(8,128)}, u32[]{:S(2)}) copy-start(f32[12,256]{1,0:T(8,128)} %get-tuple-element.75) | copy-start | bytes 36868
  572.2 122.0 %reduce-scatter.31.cloned.1.call-start = ((), (), s32[]{:S(2)}) async-start(), calls=%async_computation.25 | async-start | bytes 1474560 | tf_op jit(solution)/shard_map/reduce_scatter | solution.py:257
  588.0 106.2 %reduce-scatter.35.cloned.1.call-start = ((), (), s32[]{:S(2)}) async-start(), calls=%async_computation.27 | async-start | bytes 5898240 | tf_op jit(solution)/shard_map/reduce_scatter | solution.py:263
  602.5 137.2 %reduce-scatter.33.cloned.1.call-start = ((), (), s32[]{:S(2)}) async-start(), calls=%async_computation.26 | async-start | bytes 5898240 | tf_op jit(solution)/shard_map/reduce_scatter | solution.py:260
  619.8 163.0 %reduce-scatter.29.cloned.1.call-start = ((), (), s32[]{:S(2)}) async-start(), calls=%async_computation.24 | async-start | bytes 4423680 | tf_op jit(solution)/shard_map/reduce_scatter | solution.py:254
  645.5 160.0 %reduce-scatter.37.cloned.1.call-start = ((), (), s32[]{:S(2)}) async-start(), calls=%async_computation.28 | async-start | bytes 245760
  689.8 138.3 %reduce-scatter.39.cloned.1.call-start = ((), (), s32[]{:S(2)}) async-start(), calls=%async_computation.29 | async-start | bytes 245760
  694.1 271.5 %all-reduce.5.cloned.1.call-start = ((), (), s32[]{:S(2)}) async-start(), calls=%async_computation.30 | async-start | bytes 7077888 | tf_op jit(solution)/shard_map/psum | solution.py:277
  (173 other events, 754.4 us)
Sparse Core Ops, SparseCore 0:
  17.2 22.3 all-gather.8
  41.8 19.6 all-gather.6
  102.3 20.6 all-gather.12
  125.0 19.6 all-gather.10
  212.4 28.1 reduce-scatter.16
  243.8 28.1 reduce-scatter.18
  300.1 18.7 all-gather.16
  320.4 19.6 all-gather.14
  424.5 27.2 reduce-scatter.20
  454.9 28.1 reduce-scatter.22
  552.1 27.2 reduce-scatter.24
  582.5 28.1 reduce-scatter.26
  613.3 25.7 reduce-scatter.30
  641.6 47.8 reduce-scatter.34
  691.8 47.8 reduce-scatter.32
  742.3 40.4 reduce-scatter.28
  785.6 19.7 reduce-scatter.36
  808.3 19.7 reduce-scatter.38
  830.7 134.9 all-reduce.4
where the time goes:
time: 991 us; the launch traced here: 979 us
  waiting for transfers between devices  368 us (37%)
  matrix products  318 us (32%)
  other arithmetic  129 us (13%)
  local copies, waits for them, and re-layouts  116 us (12%)
  blocking collectives  19.3 us (2%)
  between operations  17.3 us (2%)
  starting transfers between devices  11.7 us (1%)
    psum x1, waiting for transfers between devices, body(): lax.psum(within[0].astype(jnp.bfloat16), 'group').astype(jnp.float32)  121 us
    dot_general x12, matrix products, row_contract(): lax.dot_general(left, right, (((0,), (0,)), ((), ())), preferred_element_...  77.4 us
    dot_general x12, matrix products, back_dot(): lax.dot_general(left, weight, (((1,), (1,)), ((), ())), preferred_element...  58.9 us
    reduce_scatter x1, waiting for transfers between devices, body(): lax.psum_scatter(totals[2].astype(jnp.bfloat16), 'narrow', scatter_dimens...  45.4 us
    reduce_scatter x1, waiting for transfers between devices, body(): lax.psum_scatter(totals[0].astype(jnp.bfloat16), 'narrow', scatter_dimens...  43.1 us
    reduce_scatter x3, waiting for transfers between devices, backward_layer(): lax.psum_scatter(value_part.astype(jnp.bfloat16), 'narrow', scatter_dimen...  41.6 us
    all_gather x3, waiting for transfers between devices, forward_layer(): lax.all_gather(key_rows, 'narrow', axis=0, tiled=True)  31 us
    dot_general x3, matrix products, forward_layer(): jnp.dot(activated, fc2_w, preferred_element_type=jnp.float32) + bias_rows[5]  29.7 us
  transfers between devices with their start and end apart: 23, of which 16 were waited for; matrix products, arithmetic and copies ran while one was open for 30% of the time, Pallas kernels for 0%

commit v1 on v0

--- a/solution.py
+++ b/solution.py
@@ -1,7 +1,738 @@
+import functools
+
 import jax
 import jax.numpy as jnp
 from jax import lax
+from jax.experimental import pallas as pl
+from jax.experimental.pallas import tpu as pltpu
 from jax.sharding import PartitionSpec as P
+
+SECTION, GROUP, NARROW = "section", "group", "narrow"
+HALVES = 2
+BIG = 1e30
+SLOT_ROWS = 192
+SLOT_COLS = 256
+RING = 6
+ZRING = 12
+HOP = 2
+BF = jnp.bfloat16
+F32 = jnp.float32
+MESH = pl.DeviceIdType.MESH
+
+
+def dot_nn(left, right):
+    return lax.dot_general(left, right, (((1,), (0,)), ((), ())), preferred_element_type=F32)
+
+
+def dot_nt(left, right):
+    return lax.dot_general(left, right, (((1,), (1,)), ((), ())), preferred_element_type=F32)
+
+
+def dot_tn(left, right):
+    return lax.dot_general(left, right, (((0,), (0,)), ((), ())), preferred_element_type=F32)
+
+
+def aligned(start, size, unit=128):
+    return pl.ds(pl.multiple_of(start, unit), size)
+
+
+def norm_stats(values):
+    mean = jnp.mean(values, -1, keepdims=True)
+    centered = values - mean
+    var = jnp.mean(centered * centered, -1, keepdims=True)
+    rstd = lax.rsqrt(var + 1e-06)
+    return centered * rstd, rstd
+
+
+def norm_back(grad, hat, rstd, gain):
+    scaled = grad * gain
+    mean_one = jnp.mean(scaled, -1, keepdims=True)
+    mean_two = jnp.mean(scaled * hat, -1, keepdims=True)
+    return rstd * (scaled - mean_one - hat * mean_two)
+
+
+def three_parts(column, lane, base):
+    high = column.astype(BF).astype(F32)
+    rest = column - high
+    mid = rest.astype(BF).astype(F32)
+    low = rest - mid
+    return jnp.where(
+        lane == base, high, jnp.where(lane == base + 1, mid, jnp.where(lane == base + 2, low, 0.0))
+    )
+
+
+def kernel(groups, *refs):
+    (
+        boundary, segf, wqkv_h, wproj_h, wfc1_h, wfc2_h, gains, biases, fc1b,
+        results, g_qkv, g_proj, g_fc1, g_fc2, vec_out,
+        wqkv, wproj, wfc1, wfc2,
+        hin, cot, n1, qaug, kall, vall, ob, zb, rb, n2, gp, act, mb, fout,
+        dmb, du, drb, dzb, doaug, dqkv, dkv_send, dkv_recv, dout,
+        unit, ckeep, csend, crecv, ysend, yrecv, rown, zsend, zrecv, ostage,
+        vec, dcf, vsend, vrecv,
+        w_sem, b_sem, bx_sem, kv_ssem, kv_rsem, x_ssem, x_rsem, xb_ssem, xb_rsem,
+        dkv_ssem, dkv_rsem, res_sem,
+        c_ssem, c_rsem, y_ssem, y_rsem, z_ssem, z_rsem, o_sem,
+        v_ssem, v_rsem, credit,
+    ) = refs
+    sec = lax.axis_index(SECTION)
+    grp = lax.axis_index(GROUP)
+    nar = lax.axis_index(NARROW)
+    yy = nar // 2
+    cc = nar % 2
+    sib = (sec, grp, nar + 1 - 2 * cc)
+    ynb = (sec, grp, (nar + 2) % 4)
+    xnb = (1 - sec, grp, nar)
+    zright = (sec, grp + 1, nar)
+    zleft = (sec, grp - 1, nar)
+    has_right = grp < groups - 1
+    has_left = grp > 0
+    is_first = sec == 0
+    is_second = sec == 1
+
+    blk = boundary.shape[2]
+    rows = 2 * blk
+    width = boundary.shape[3]
+    ff = wfc1.shape[1]
+    pairs = width // 128
+    chunks = rows // blk
+
+    weight_copies = [
+        pltpu.make_async_copy(src.at[0], dst, w_sem.at[i])
+        for i, (src, dst) in enumerate(
+            ((wqkv_h, wqkv), (wproj_h, wproj), (wfc1_h, wfc1), (wfc2_h, wfc2))
+        )
+    ]
+    for copy in weight_copies:
+        copy.start()
+
+    def own_block(dst):
+        return pltpu.make_async_copy(boundary.at[0, yy], dst.at[aligned(yy * blk, blk)], b_sem)
+
+    def swap_block(dst):
+        return pltpu.make_async_remote_copy(
+            src_ref=boundary.at[0, 1 - yy],
+            dst_ref=dst.at[aligned(yy * blk, blk)],
+            send_sem=bx_sem.at[0],
+            recv_sem=bx_sem.at[1],
+            device_id=ynb,
+            device_id_type=MESH,
+        )
+
+    @pl.when(is_first)
+    def _():
+        own_block(hin).start()
+
+    @pl.when(is_second)
+    def _():
+        own_block(cot).start()
+
+    barrier = pltpu.get_barrier_semaphore()
+    for peer in (sib, ynb, xnb):
+        pl.semaphore_signal(barrier, inc=1, device_id=peer, device_id_type=MESH)
+
+    @pl.when(has_right)
+    def _():
+        pl.semaphore_signal(barrier, inc=1, device_id=zright, device_id_type=MESH)
+
+    @pl.when(has_left)
+    def _():
+        pl.semaphore_signal(barrier, inc=1, device_id=zleft, device_id_type=MESH)
+
+    pl.semaphore_wait(barrier, 3 + has_right.astype(jnp.int32) + has_left.astype(jnp.int32))
+
+    @pl.when(is_first)
+    def _():
+        swap_block(hin).start()
+
+    @pl.when(is_second)
+    def _():
+        swap_block(cot).start()
+
+    vec[...] = jnp.zeros_like(vec)
+    dcf[...] = jnp.zeros_like(dcf)
+
+    lane_row = lax.broadcasted_iota(jnp.int32, (1, 128), 1)
+    first_row = jnp.where(lane_row < 64, 1.0, 0.0).astype(BF)
+    second_row = jnp.where(lane_row < 64, 0.0, 1.0).astype(BF)
+    half_lane = lax.rem(lane_row, 64)
+    penalty_row = jnp.where(half_lane < 4, BIG, 0.0)
+
+    def x_send(dst, src, j, ssem, rsem):
+        part = pl.ds(j * blk, blk)
+        return pltpu.make_async_remote_copy(
+            src_ref=src.at[part],
+            dst_ref=dst.at[part],
+            send_sem=ssem.at[j],
+            recv_sem=rsem.at[j],
+            device_id=xnb,
+            device_id_type=MESH,
+        )
+
+    def kv_copy(which, j):
+        ref = (kall, vall)[which]
+        start = pl.multiple_of(j * blk, blk)
+        return pltpu.make_async_remote_copy(
+            src_ref=ref.at[pl.ds(start, blk)],
+            dst_ref=ref.at[pl.ds(start + rows, blk)],
+            send_sem=kv_ssem.at[which, j],
+            recv_sem=kv_rsem.at[which, j],
+            device_id=sib,
+            device_id_type=MESH,
+        )
+
+    for j in range(chunks):
+        @pl.when(is_first)
+        def _():
+            if j == 0:
+                own_block(hin).wait()
+            else:
+                swap_block(hin).wait()
+
+        @pl.when(is_second)
+        def _():
+            x_send(hin, fout, j, x_ssem, x_rsem).wait_recv()
+
+        block = jnp.where(is_first, (yy + j) % 2, j)
+        part = aligned(block * blk, blk)
+        hat, _ = norm_stats(hin[part, :].astype(F32))
+        n1[part, :] = (hat * gains[0, 0:1, :] + biases[0, 0:1, :]).astype(BF)
+        if j == 0:
+            weight_copies[0].wait()
+
+        def project(t, carry, part=part):
+            cols = aligned(t * 256, 256)
+            got = dot_nn(n1[part, :], wqkv[:, cols])
+
+            @pl.when(t < 3)
+            def _():
+                low = ((got + biases[0, 1:2, cols]).astype(BF) * 0.125).astype(F32)
+                penalty = (segf[part, :].astype(F32) - 1.0) * penalty_row
+                for i in range(2):
+                    pair = low[:, i * 128 : (i + 1) * 128]
+                    qaug[t * 4 + 2 * i, part, :] = jnp.where(lane_row < 64, pair, penalty).astype(BF)
+                    qaug[t * 4 + 2 * i + 1, part, :] = jnp.where(lane_row < 64, penalty, pair).astype(BF)
+
+            @pl.when((t >= 3) & (t < 6))
+            def _():
+                kall[part, aligned(t * 256 - width, 256)] = got.astype(BF)
+
+            @pl.when(t >= 6)
+            def _():
+                at = aligned(t * 256 - 2 * width, 256)
+                vall[part, at] = (got + biases[0, 2:3, at]).astype(BF)
+
+            return carry
+
+        lax.fori_loop(3, 9, project, 0)
+        kv_copy(0, block).start()
+        kv_copy(1, block).start()
+        lax.fori_loop(0, 3, project, 0)
+
+    for j in range(chunks):
+        kv_copy(0, j).wait()
+        kv_copy(1, j).wait()
+
+    def aug_pair(pair):
+        cols = aligned(pair * 128, 128)
+        keys, values, feats = kall[:, cols], vall[:, cols], segf[...]
+        feat_a, feat_b = feats * second_row, feats * first_row
+        return (
+            (keys * first_row + feat_a, values * first_row + feat_a),
+            (keys * second_row + feat_b, values * second_row + feat_b),
+        )
+
+    def forward_block(j, carry):
+        part = aligned(j * blk, blk)
+
+        def attend(pair, carry):
+            outs = []
+            for i, (keys, values) in enumerate(aug_pair(pair)):
+                base = 64 * (1 - i)
+                query = qaug[2 * pair + i, part, :]
+                scores = dot_nt(query, keys)
+                peak = jnp.max(scores, -1, keepdims=True)
+                expo = jnp.exp(scores - peak).astype(BF)
+                mixed = dot_nn(expo, values)
+                total = mixed[:, base + 4 : base + 5]
+                outs.append(mixed / total)
+                log_total = peak + jnp.log(total)
+                extra = three_parts(-log_total, lane_row, base + 4)
+                qaug[2 * pair + i, part, :] = (query.astype(F32) + extra).astype(BF)
+            ob[part, aligned(pair * 128, 128)] = jnp.where(lane_row < 64, outs[0], outs[1]).astype(BF)
+            return carry
+
+        lax.fori_loop(0, pairs, attend, 0)
+
+        if j == 0:
+            for copy in weight_copies[1:]:
+                copy.wait()
+
+        branch = dot_nn(ob[part, :], wproj[...]) + biases[0, 3:4, :]
+        zb[part, :] = branch.astype(BF)
+        middle = hin[part, :].astype(F32) + gains[0, 1:2, :] * branch
+        rb[part, :] = middle
+        hat, _ = norm_stats(middle)
+        n2[part, :] = (hat * gains[0, 2:3, :] + biases[0, 4:5, :]).astype(BF)
+
+        def expand(t, carry):
+            cols = aligned(t * 256, 256)
+            pre = dot_nn(n2[part, :], wfc1[:, cols]) + fc1b[0:1, cols]
+            phi = 0.5 + 0.5 * lax.erf(pre * 0.7071067811865476)
+            act[part, cols] = (pre * phi).astype(BF)
+            slope = phi + pre * (jnp.exp(-0.5 * pre * pre) * 0.3989422804014327)
+            gp[part, cols] = slope.astype(BF)
+            return carry
+
+        lax.fori_loop(0, ff // 256, expand, 0)
+        mlp = dot_nn(act[part, :], wfc2[...]) + biases[0, 5:6, :]
+        mb[part, :] = mlp.astype(BF)
+        fout[part, :] = (rb[part, :] + gains[0, 3:4, :] * mlp).astype(BF)
+        return carry
+
+    for j in range(chunks):
+        forward_block(j, 0)
+
+        @pl.when(is_first)
+        def _():
+            x_send(hin, fout, j, x_ssem, x_rsem).start()
+
+    @pl.when(is_second)
+    def _():
+        own_block(cot).wait()
+        swap_block(cot).wait()
+
+    for j in range(chunks):
+        part = pl.ds(j * blk, blk)
+
+        @pl.when(is_first)
+        def _():
+            x_send(cot, dout, j, xb_ssem, xb_rsem).wait_recv()
+
+        grad = cot[part, :].astype(F32)
+        vec[3:4, :] += jnp.sum(grad * mb[part, :].astype(F32), 0, keepdims=True)
+        low = (gains[0, 3:4, :] * grad).astype(BF)
+        dmb[part, :] = low
+        vec[9:10, :] += jnp.sum(low.astype(F32), 0, keepdims=True)
+
+    def shrink(t, carry):
+        cols = aligned(t * 256, 256)
+        back = dot_nt(dmb[...], wfc2[cols, :])
+        low = (gp[:, cols].astype(F32) * back).astype(BF)
+        du[:, cols] = low
+        dcf[pl.ds(t, 1), :] = jnp.sum(low.astype(F32), 0, keepdims=True)
+        return carry
+
+    lax.fori_loop(0, ff // 256, shrink, 0)
+
+    for j in range(chunks):
+        part = pl.ds(j * blk, blk)
+        grad_two = dot_nt(du[part, :], wfc1[...])
+        hat, rstd = norm_stats(rb[part, :])
+        vec[2:3, :] += jnp.sum(grad_two * hat, 0, keepdims=True)
+        vec[8:9, :] += jnp.sum(grad_two, 0, keepdims=True)
+        middle = cot[part, :].astype(F32) + norm_back(grad_two, hat, rstd, gains[0, 2:3, :])
+        drb[part, :] = middle
+        vec[1:2, :] += jnp.sum(middle * zb[part, :].astype(F32), 0, keepdims=True)
+        low = (gains[0, 1:2, :] * middle).astype(BF)
+        dzb[part, :] = low
+        vec[7:8, :] += jnp.sum(low.astype(F32), 0, keepdims=True)
+
+        def heads(t, carry, part=part):
+            cols = aligned(t * 256, 256)
+            grad_o = dot_nt(dzb[part, :], wproj[cols, :]).astype(BF)
+            prod = grad_o.astype(F32) * ob[part, cols].astype(F32)
+            for i in range(2):
+                pair = grad_o[:, i * 128 : (i + 1) * 128].astype(F32)
+                both = prod[:, i * 128 : (i + 1) * 128]
+                inner_a = jnp.sum(jnp.where(lane_row < 64, both, 0.0), -1, keepdims=True)
+                inner_b = jnp.sum(jnp.where(lane_row < 64, 0.0, both), -1, keepdims=True)
+                extra_a = three_parts(-inner_a, lane_row, 68)
+                extra_b = three_parts(-inner_b, lane_row, 4)
+                doaug[t * 4 + 2 * i, part, :] = jnp.where(lane_row < 64, pair, extra_a).astype(BF)
+                doaug[t * 4 + 2 * i + 1, part, :] = jnp.where(lane_row < 64, extra_b, pair).astype(BF)
+            return carry
+
+        lax.fori_loop(0, width // 256, heads, 0)
+
+    def dkv_copy(index):
+        return pltpu.make_async_remote_copy(
+            src_ref=dkv_send.at[index],
+            dst_ref=dkv_recv.at[index],
+            send_sem=dkv_ssem.at[index],
+            recv_sem=dkv_rsem.at[index],
+            device_id=sib,
+            device_id_type=MESH,
+        )
+
+    def attend_back(pair, carry):
+        sides = aug_pair(pair)
+        grads = {}
+        for i, (keys, values) in enumerate(sides):
+            query = qaug[2 * pair + i]
+            outer = doaug[2 * pair + i]
+            for half in (1, 0):
+                span = slice(half * rows, (half + 1) * rows)
+                prob = jnp.exp(dot_nt(keys[span], query))
+                diff = dot_nt(values[span], outer)
+                slope = (prob * diff).astype(BF)
+                grads["v", i, half] = dot_nn(prob.astype(BF), outer)
+                grads["k", i, half] = dot_nn(slope, query)
+                grads["q", i, half] = dot_tn(slope, keys[span])
+        cols = aligned(pair * 128, 128)
+
+        def merged(name, half):
+            return jnp.where(lane_row < 64, grads[name, 0, half], grads[name, 1, half])
+
+        dkv_send[pair] = merged("k", 1).astype(BF)
+        dkv_send[pairs + pair] = merged("v", 1).astype(BF)
+        dkv_copy(pair).start()
+        dkv_copy(pairs + pair).start()
+        dqkv[:, cols] = ((merged("q", 0) + merged("q", 1)) * 0.125).astype(BF)
+        dqkv[:, aligned(width + pair * 128, 128)] = merged("k", 0).astype(BF)
+        dqkv[:, aligned(2 * width + pair * 128, 128)] = merged("v", 0).astype(BF)
+        return carry
+
+    lax.fori_loop(0, pairs, attend_back, 0)
+
+    def collect(index, carry):
+        dkv_copy(index).wait()
+        cols = aligned(width + index * 128, 128)
+        dqkv[:, cols] = (dqkv[:, cols].astype(F32) + dkv_recv[index].astype(F32)).astype(BF)
+        return carry
+
+    lax.fori_loop(0, 2 * pairs, collect, 0)
+
+    for j in range(chunks):
+        part = pl.ds(j * blk, blk)
+        vec[5:6, :] += jnp.sum(dqkv[part, 0:width].astype(F32), 0, keepdims=True)
+        vec[6:7, :] += jnp.sum(dqkv[part, 2 * width : 3 * width].astype(F32), 0, keepdims=True)
+        grad_one = dot_nt(dqkv[part, :], wqkv[...])
+        hat, rstd = norm_stats(hin[part, :].astype(F32))
+        vec[0:1, :] += jnp.sum(grad_one * hat, 0, keepdims=True)
+        vec[4:5, :] += jnp.sum(grad_one, 0, keepdims=True)
+        total = drb[part, :] + norm_back(grad_one, hat, rstd, gains[0, 0:1, :])
+        dout[part, :] = total.astype(BF)
+
+        @pl.when(is_second)
+        def _():
+            x_send(cot, dout, j, xb_ssem, xb_rsem).start()
+
+    n_fc2 = 2 * (width // 128)
+    n_fc1 = ff // SLOT_COLS
+    n_proj = width // SLOT_COLS
+    n_qkv = 3 * width // SLOT_COLS
+    lo_fc1 = n_fc2
+    lo_proj = lo_fc1 + n_fc1
+    lo_qkv = lo_proj + n_proj
+    slots = lo_qkv + n_qkv
+    vslot = slots - 6
+    d_core = 1
+    d_y = 3
+    d_z = d_y + 1
+
+    def core_copy(t):
+        at = t % RING
+        return pltpu.make_async_remote_copy(
+            src_ref=csend.at[at], dst_ref=crecv.at[at],
+            send_sem=c_ssem.at[at], recv_sem=c_rsem.at[at],
+            device_id=sib, device_id_type=MESH,
+        )
+
+    def y_copy(t):
+        at = t % RING
+        return pltpu.make_async_remote_copy(
+            src_ref=ysend.at[at], dst_ref=yrecv.at[at],
+            send_sem=y_ssem.at[at], recv_sem=y_rsem.at[at],
+            device_id=ynb, device_id_type=MESH,
+        )
+
+    def z_copy(way, t):
+        return pltpu.make_async_remote_copy(
+            src_ref=zsend.at[way, t % RING], dst_ref=zrecv.at[way, t % ZRING],
+            send_sem=z_ssem.at[way, t % RING], recv_sem=z_rsem.at[way, t % ZRING],
+            device_id=(zright, zleft)[way], device_id_type=MESH,
+        )
+
+    def v_copy(stage, peer):
+        return pltpu.make_async_remote_copy(
+            src_ref=vsend.at[stage], dst_ref=vrecv.at[stage],
+            send_sem=v_ssem.at[stage], recv_sem=v_rsem.at[stage],
+            device_id=peer, device_id_type=MESH,
+        )
+
+    def give(which, t, depth, peer):
+        @pl.when(t + depth < slots)
+        def _():
+            pl.semaphore_signal(credit.at[which], inc=1, device_id=peer, device_id_type=MESH)
+
+    def take(which, t, depth):
+        @pl.when(t >= depth)
+        def _():
+            pl.semaphore_wait(credit.at[which], 1)
+
+    def out_copies(t, action):
+        src = ostage.at[t % 4]
+
+        @pl.when(t < lo_fc1)
+        def _():
+            row = (t // (width // 128)) * (2 * SLOT_ROWS)
+            cols = aligned((t % (width // 128)) * 128, 128)
+            for i in range(2):
+                action(pltpu.make_async_copy(
+                    src.at[:, i * 128 : (i + 1) * 128],
+                    g_fc2.at[pl.ds(pl.multiple_of(row + i * SLOT_ROWS, SLOT_ROWS), SLOT_ROWS), cols],
+                    o_sem.at[t % 4, i],
+                ))
+
+        for lo, count, ref in ((lo_fc1, n_fc1, g_fc1), (lo_proj, n_proj, g_proj), (lo_qkv, n_qkv, g_qkv)):
+            @pl.when((t >= lo) & (t < lo + count))
+            def _():
+                action(pltpu.make_async_copy(src, ref.at[:, aligned((t - lo) * SLOT_COLS, SLOT_COLS)], o_sem.at[t % 4, 0]))
+
+    def result_copies(action):
+        for flag, src in ((is_first, dout), (is_second, fout)):
+            @pl.when(flag)
+            def _():
+                action(pltpu.make_async_copy(
+                    src.at[aligned(yy * blk, blk)], results.at[yy], res_sem.at[0]
+                ))
+                action(pltpu.make_async_remote_copy(
+                    src_ref=src.at[aligned((1 - yy) * blk, blk)], dst_ref=results.at[yy],
+                    send_sem=res_sem.at[1], recv_sem=res_sem.at[2],
+                    device_id=ynb, device_id_type=MESH,
+                ))
+
+    def step(s, carry):
+        @pl.when(s < slots)
+        def _():
+            take(0, s, RING)
+
+            @pl.when(s >= RING)
+            def _():
+                core_copy(s - RING).wait_send()
+
+            at = s % RING
+            keep = s % 2
+
+            @pl.when(s < lo_fc1)
+            def _():
+                row = (s // (width // 128)) * (2 * SLOT_ROWS)
+                cols = aligned((s % (width // 128)) * 128, 128)
+                for side in range(2):
+                    for core in range(2):
+                        first = (2 * side + core) * width + row
+                        got = dot_tn(act[:, aligned(first, 2 * SLOT_ROWS)], dmb[:, cols])
+
+                        @pl.when(cc == core)
+                        def _():
+                            for i in range(2):
+                                ckeep[keep, side, :, i * 128 : (i + 1) * 128] = got[i * SLOT_ROWS : (i + 1) * SLOT_ROWS]
+
+                        @pl.when(cc != core)
+                        def _():
+                            for i in range(2):
+                                csend[at, side, :, i * 128 : (i + 1) * 128] = got[i * SLOT_ROWS : (i + 1) * SLOT_ROWS].astype(BF)
+
+            for lo, count, left, right in (
+                (lo_fc1, n_fc1, n2, du), (lo_proj, n_proj, ob, dzb), (lo_qkv, n_qkv, n1, dqkv)
+            ):
+                @pl.when((s >= lo) & (s < lo + count))
+                def _():
+                    cols = aligned((s - lo) * SLOT_COLS, SLOT_COLS)
+                    for side in range(2):
+                        unit[...] = dot_tn(left[:, side * 2 * SLOT_ROWS : (side + 1) * 2 * SLOT_ROWS], right[:, cols])
+                        ckeep[keep, side] = unit[pl.ds(pl.multiple_of(cc * SLOT_ROWS, SLOT_ROWS), SLOT_ROWS), :]
+                        csend[at, side] = unit[pl.ds(pl.multiple_of((1 - cc) * SLOT_ROWS, SLOT_ROWS), SLOT_ROWS), :].astype(BF)
+
+            core_copy(s).start()
+
+            @pl.when(s == vslot)
+            def _():
+                vsend[0, :, 0:width] = vec[...]
+                vsend[0, :, width : width + 256] = dcf[...]
+                v_copy(0, sib).start()
+
+        t = s - d_core
+
+        @pl.when((t >= 0) & (t < slots))
+        def _():
+            core_copy(t).wait_recv()
+            at = t % RING
+            keep = t % 2
+            take(1, t, RING)
+
+            @pl.when(t >= RING)
+            def _():
+                y_copy(t - RING).wait_send()
+
+            away = 1 - yy
+            ysend[at] = (ckeep[keep, away] + crecv[at, away].astype(F32)).astype(BF)
+            y_copy(t).start()
+            rown[t % ZRING] = ckeep[keep, yy] + crecv[at, yy].astype(F32)
+            give(0, t, RING, sib)
+
+            @pl.when(t == vslot)
+            def _():
+                v_copy(0, sib).wait()
+                vsend[1] = vsend[0] + vrecv[0]
+                v_copy(1, ynb).start()
+
+        t = s - d_y
+
+        @pl.when((t >= 0) & (t < slots))
+        def _():
+            y_copy(t).wait_recv()
+            at = t % ZRING
+            rown[at] = rown[at] + yrecv[t % RING].astype(F32)
+            give(1, t, RING, ynb)
+
+            @pl.when(t == vslot)
+            def _():
+                v_copy(1, ynb).wait()
+                vsend[2] = vsend[1] + vrecv[1]
+
+        for way in range(2):
+            place = grp if way == 0 else groups - 1 - grp
+            has_before = place > 0
+            has_after = place < groups - 1
+            behind = (zleft, zright)[way]
+            ahead = (zright, zleft)[way]
+            t = s - d_z - place * HOP
+            inside = (t >= 0) & (t < slots)
+
+            @pl.when(inside & has_before)
+            def _():
+                z_copy(way, t).wait_recv()
+
+            @pl.when(inside & has_after)
+            def _():
+                take(2 + way, t, ZRING)
+
+                @pl.when(t >= RING)
+                def _():
+                    z_copy(way, t - RING).wait_send()
+
+                @pl.when(has_before)
+                def _():
+                    zsend[way, t % RING] = (rown[t % ZRING] + zrecv[way, t % ZRING].astype(F32)).astype(BF)
+
+                @pl.when(jnp.logical_not(has_before))
+                def _():
+                    zsend[way, t % RING] = rown[t % ZRING].astype(BF)
+
+                z_copy(way, t).start()
+
+            @pl.when(t == vslot)
+            def _():
+                @pl.when(has_before)
+                def _():
+                    v_copy(2 + way, behind).wait_recv()
+
+                @pl.when(has_after)
+                def _():
+                    @pl.when(has_before)
+                    def _():
+                        vsend[3 + way] = vsend[2] + vrecv[2 + way]
+
+                    @pl.when(jnp.logical_not(has_before))
+                    def _():
+                        vsend[3 + way] = vsend[2]
+
+                    v_send(way, ahead).start()
+
+        late = jnp.maximum(grp, groups - 1 - grp)
+        t = s - d_z - late * HOP
+
+        @pl.when((t >= 0) & (t < slots))
+        def _():
+            at = t % ZRING
+
+            @pl.when(t >= 4)
+            def _():
+                out_copies(t - 4, lambda copy: copy.wait())
+
+            @pl.when(has_left & has_right)
+            def _():
+                ostage[t % 4] = (rown[at] + zrecv[0, at].astype(F32) + zrecv[1, at].astype(F32)).astype(BF)
+
+            @pl.when(has_left & jnp.logical_not(has_right))
+            def _():
+                ostage[t % 4] = (rown[at] + zrecv[0, at].astype(F32)).astype(BF)
+
+            @pl.when(has_right & jnp.logical_not(has_left))
+            def _():
+                ostage[t % 4] = (rown[at] + zrecv[1, at].astype(F32)).astype(BF)
+
+            out_copies(t, lambda copy: copy.start())
+
+            @pl.when(has_left)
+            def _():
+                give(2, t, ZRING, zleft)
+
+            @pl.when(has_right)
+            def _():
+                give(3, t, ZRING, zright)
+
+        @pl.when(s == slots + d_core)
+        def _():
+            result_copies(lambda copy: copy.start())
+
+        return carry
+
+    def v_send(way, peer):
+        return pltpu.make_async_remote_copy(
+            src_ref=vsend.at[3 + way], dst_ref=vrecv.at[2 + way],
+            send_sem=v_ssem.at[2 + way], recv_sem=v_rsem.at[2 + way],
+            device_id=peer, device_id_type=MESH,
+        )
+
+    steps = slots + d_z + (groups - 1) * HOP
+    lax.fori_loop(0, steps, step, 0)
+
+    for t in range(slots - 4, slots):
+        out_copies(t, lambda copy: copy.wait())
+    for t in range(slots - RING, slots):
+        core_copy(t).wait_send()
+        y_copy(t).wait_send()
+
+        @pl.when(has_right)
+        def _():
+            z_copy(0, t).wait_send()
+
+        @pl.when(has_left)
+        def _():
+            z_copy(1, t).wait_send()
+
+    @pl.when(has_right)
+    def _():
+        v_send(0, zright).wait_send()
+
+    @pl.when(has_left)
+    def _():
+        v_send(1, zleft).wait_send()
+
+    total = vsend[2]
+    vec_out[...] = total
+
+    @pl.when(has_left)
+    def _():
+        vec_out[...] = vec_out[...] + vrecv[2]
+
+    @pl.when(has_right)
+    def _():
+        vec_out[...] = vec_out[...] + vrecv[3]
+
+    for j in range(chunks):
+        @pl.when(is_first)
+        def _():
+            x_send(hin, fout, j, x_ssem, x_rsem).wait_send()
+
+        @pl.when(is_second)
+        def _():
+            x_send(cot, dout, j, xb_ssem, xb_rsem).wait_send()
+
+    result_copies(lambda copy: copy.wait())
 
 HEADS = 12
 HDIM = 64
@@ -195,7 +926,7 @@
     )
 
 
-def body(
+def general_body(
     boundary, segments, qkv_weight, proj_weight, fc1_weight, fc2_weight, gains, biases, fc1_bias
 ):
     weights = (
@@ -294,7 +1025,86 @@
     )
 
 
+def segment_features(seg_row, blk, core):
+    parts = seg_row.reshape(HALVES, 2, blk)
+    ordered = jnp.concatenate([parts[:, core].reshape(-1), parts[:, 1 - core].reshape(-1)])
+    lane = jnp.arange(128) % 64
+    hot = (ordered[:, None] == lane[None, :]) & (lane < 4)[None, :]
+    ones = (lane >= 4) & (lane < 7)
+    return (hot | ones[None, :]).astype(BF)
+
+
+def fused_body(
+    groups, boundary, segments, qkv_weight, proj_weight, fc1_weight, fc2_weight, gains, biases, fc1_bias
+):
+    blk, width = boundary.shape[2:]
+    rows, keys = 2 * blk, 4 * blk
+    ff = fc1_weight.shape[2]
+    heads = width // HDIM
+    nar = lax.axis_index(NARROW)
+    seg_row = lax.dynamic_index_in_dim(segments, nar // 2, 0, keepdims=False)
+    feats = segment_features(seg_row, blk, nar % 2)
+
+    def bf(*shape):
+        return pltpu.VMEM(shape, BF)
+
+    def f32(*shape):
+        return pltpu.VMEM(shape, F32)
+
+    dma = pltpu.SemaphoreType.DMA
+    slot = (SLOT_ROWS, SLOT_COLS)
+    scratch = [
+        bf(width, 3 * width), bf(width, width), bf(width, ff), bf(ff, width),
+        bf(rows, width), bf(rows, width), bf(rows, width), bf(heads, rows, 128),
+        bf(keys, width), bf(keys, width), bf(rows, width), bf(rows, width),
+        f32(rows, width), bf(rows, width), bf(rows, ff), bf(rows, ff), bf(rows, width), bf(rows, width),
+        bf(rows, width), bf(rows, ff), f32(rows, width), bf(rows, width), bf(heads, rows, 128),
+        bf(rows, 3 * width), bf(heads, rows, 128), bf(heads, rows, 128), bf(rows, width),
+        f32(2 * SLOT_ROWS, SLOT_COLS), f32(2, 2, *slot), bf(RING, 2, *slot), bf(RING, 2, *slot),
+        bf(RING, *slot), bf(RING, *slot), f32(ZRING, *slot), bf(2, RING, *slot), bf(2, ZRING, *slot), bf(4, *slot),
+        f32(16, width), f32(16, 256), f32(5, 16, width + 256), f32(4, 16, width + 256),
+        dma((4,)), dma(()), dma((2,)), dma((2, 2)), dma((2, 2)), dma((2,)), dma((2,)), dma((2,)), dma((2,)),
+        dma((heads,)), dma((heads,)), dma((3,)),
+        dma((RING,)), dma((RING,)), dma((RING,)), dma((RING,)), dma((2, RING)), dma((2, ZRING)), dma((4, 2)),
+        dma((4,)), dma((4,)), pltpu.SemaphoreType.REGULAR((4,)),
+    ]
+    hbm = pl.BlockSpec(memory_space=pl.ANY)
+    vmem = pl.BlockSpec(memory_space=pltpu.VMEM)
+    out = pl.pallas_call(
+        functools.partial(kernel, groups),
+        out_shape=(
+            jax.ShapeDtypeStruct((2, blk, width), BF),
+            jax.ShapeDtypeStruct((width // 4, 3 * width), BF),
+            jax.ShapeDtypeStruct((width // 4, width), BF),
+            jax.ShapeDtypeStruct((width // 4, ff), BF),
+            jax.ShapeDtypeStruct((ff // 4, width), BF),
+            jax.ShapeDtypeStruct((16, width + 256), F32),
+        ),
+        in_specs=[hbm, vmem, hbm, hbm, hbm, hbm, vmem, vmem, vmem],
+        out_specs=(hbm, hbm, hbm, hbm, hbm, vmem),
+        scratch_shapes=scratch,
+        compiler_params=pltpu.CompilerParams(
+            collective_id=0, has_side_effects=True, vmem_limit_bytes=63 * 2**20
+        ),
+        name="two_layers",
+    )(boundary, feats, qkv_weight, proj_weight, fc1_weight, fc2_weight, gains, biases, fc1_bias)
+    results, qkv, proj, fc1, fc2, vecs = out
+    share = lax.dynamic_slice_in_dim(vecs[:, :width], nar * (width // 4), width // 4, 1)
+    fc1_share = lax.dynamic_slice_in_dim(vecs[: ff // 256, width:].reshape(-1), nar * (ff // 4), ff // 4, 0)
+    return (
+        results[None],
+        qkv.astype(F32)[None],
+        proj.astype(F32)[None],
+        fc1.astype(F32)[None],
+        fc2.astype(F32)[None],
+        share[:4][None],
+        share[4:10][None],
+        fc1_share[None],
+    )
+
+
 def solution(mesh):
+    sections, groups, narrow = (mesh.shape[name] for name in (SECTION, GROUP, NARROW))
     placed = (
         P("section", "group", "narrow", None),
         P("group", None),
@@ -306,6 +1116,8 @@
         P("section", None, None),
         P("section", None),
     )
+    fused = sections == 2 and narrow == 4 and groups > 1
+    body = functools.partial(fused_body, groups) if fused else general_body
     return jax.shard_map(
         body,
         mesh=mesh,

time: 991 us -> 292 us (0.29); the launches traced: 979 us -> 292 us
  waiting for transfers between devices: 368 us -> 0 us
  matrix products: 318 us -> 0 us
  Pallas kernels: 0 us -> 279 us
  other arithmetic: 129 us -> 7.71 us
  local copies, waits for them, and re-layouts: 116 us -> 4.95 us
  blocking collectives: 19.3 us -> 0 us
  between operations: 17.3 us -> 0.74 us
  starting transfers between devices: 11.7 us -> 0 us
    dot_general x57 -> x0, matrix products: 318 us -> none  [the longest x12 77.4 us: row_contract(): lax.dot_general(left, right, (((0,), (0,)), ((), ())), preferred_element_...]
    pallas_call x0 -> x1, Pallas kernels: none -> 279 us  [fused_body(): pl.pallas_call(functools.partial(kernel, groups), out_shape=(jax.ShapeDty...]
    reduce_scatter x10 -> x0, waiting for transfers between devices: 130 us -> none  [the longest x1 45.4 us: body(): lax.psum_scatter(totals[2].astype(jnp.bfloat16), 'narrow', scatter_dimens...]
    psum x1 -> x0, waiting for transfers between devices: 121 us -> none  [body(): lax.psum(within[0].astype(jnp.bfloat16), 'group').astype(jnp.float32)]
    all_gather x6 -> x0, waiting for transfers between devices: 59.9 us -> none  [the longest x3 31 us: forward_layer(): lax.all_gather(key_rows, 'narrow', axis=0, tiled=True)]
    reduce_sum x34 -> x0, other arithmetic: 48.4 us -> none  [the longest x3 10.5 us: forward_layer(): jnp.sum(jnp.exp(scores - peak), -1, keepdims=True)]
    unnamed x21 -> x0, waiting for transfers between devices: 29.6 us -> none
    convert_element_type x9 -> x1, other arithmetic: 29.2 us -> 0.91 us  [segment_features(): return (hot | ones[None, :]).astype(BF)]
  transfers between devices with their start and end apart: 23 -> 0, of which waited for: 16 -> 0; matrix products, arithmetic and copies ran while one was open for 30% -> 0% of each run, Pallas kernels for 0% -> 0%
where the time goes in v1:
time: 292 us
  Pallas kernels  279 us (96%)
  other arithmetic  7.71 us (3%)
  local copies, waits for them, and re-layouts  4.95 us (2%)
    pallas_call x1, Pallas kernels, fused_body(): pl.pallas_call(functools.partial(kernel, groups), out_shape=(jax.ShapeDty...  279 us

profile of v1, /device:TPU:0, one launch (start us, length us, event | category | flops | bytes accessed | tf_op | source)
XLA Modules:
  0.0 292.2 jit_solution(5541860488723956200)
XLA Ops:
  0.6 0.0 copy-start
  0.7 0.7 copy-done
  1.4 0.9 or_convert_fusion.refs_1_
  2.3 1.3 copy.17.refs_7_
  3.7 278.8 %two_layers.1 = (bf16[2,256,768]{2,1,0:T(8,128)(2,1)}, bf16[192,2304]{1,0:T(8,128)(2,1)}, bf16[192,768]{1,0:T(8,128)(2,1)}, bf16[192,3072]{1,0:T(8,128)(2,1)}, b...) custom-call(bf16[1,2,256,768]{3,2,1,0:T(8,128)(2,1)} %refs_0_.1, bf16[1024,128]{1,0:T(8,128)(2,1)} %or_convert_fusion.refs_1_, ...), custom_call_target="tpu_custom_call" | custom-call | tf_op jit(solution)/shard_map/two_layers/pallas_call | solution.py:1073
  282.5 0.0 copy-start.1
  282.5 2.9 %bitcast_convert_fusion = f32[1,768,768]{2,1,0:T(8,128)} fusion(bf16[768,768]{1,0:T(8,128)(2,1)} %get-tuple-element.18), kind=kLoop, calls=%fused_computation | loop fusion | flops 589824 | bytes 3538944 | tf_op jit(solution)/shard_map/broadcast_in_dim | solution.py:1099
  285.5 0.0 copy-start.2
  285.5 0.0 copy-done.1
  285.5 0.0 copy-start.4
  285.5 1.7 bitcast_convert_fusion.1
  287.1 0.0 copy-start.5
  287.1 0.0 copy-start.3
  287.1 0.0 copy-done.2
  287.1 1.3 bitcast_convert_fusion.2
  288.5 0.0 copy-done.4
  288.5 0.9 bitcast_convert_fusion.3
  289.3 0.0 copy-done.5
  289.3 0.1 dynamic-slice_bitcast_fusion
  289.4 0.6 copy.18
  290.0 0.7 dynamic-slice_bitcast_fusion.1
  290.7 0.1 dynamic_slice.20
  290.8 0.6 broadcast_in_dim.51
  291.3 0.0 copy-done.3
  291.3 0.9 copy.20
  (9 shorter events, 0.1 us)
Async XLA Ops:
  0.6 0.7 copy-start
  282.5 3.0 %copy-start.1 = (bf16[192,3072]{1,0:T(8,128)(2,1)S(1)}, bf16[192,3072]{1,0:T(8,128)(2,1)}, u32[]{:S(2)}) copy-start(bf16[192,3072]{1,0:T(8,128)(2,1)} %get-tuple-element.17) | copy-start | bytes 3538948
  285.5 1.7 copy-start.2
  285.5 3.0 %copy-start.4 = (bf16[192,768]{1,0:T(8,128)(2,1)S(1)}, bf16[192,768]{1,0:T(8,128)(2,1)}, u32[]{:S(2)}) copy-start(bf16[192,768]{1,0:T(8,128)(2,1)} %get-tuple-element.16) | copy-start | bytes 884740
  287.1 2.2 copy-start.5
  287.1 4.2 %copy-start.3 = (bf16[2,256,768]{2,1,0:T(8,128)(2,1)S(1)}, bf16[2,256,768]{2,1,0:T(8,128)(2,1)}, u32[]{:S(2)}) copy-start(bf16[2,256,768]{2,1,0:T(8,128)(2,1)} %get-tuple-element.14) | copy-start | bytes 2359300
